TPU v7x, 256 devices: a whole 4x4x8 slice. The times are simulated.
256 devices in a mesh: lat: 16 (over z, core), lon: 16 (over x, y).
Axes of the slice: x: 4, y: 4, z: 8, core: 2. Of those that a mesh axis runs over, the one named last changes fastest.
Arguments:
- fields: bfloat16 [6, 72, 512, 2048], P(None, None, 'lat', 'lon'), may hold values from -6 to 6
- frac_lat: float32 [72, 16, 512], P(None, 'lon', 'lat'), may hold values from 0 to 1
- off_lat: int32 [72, 16, 512], P(None, 'lon', 'lat'), may hold values from -7 to 6
- frac_lon: float32 [72, 16, 2048], P(None, 'lat', 'lon'), may hold values from 0 to 1
- off_lon: int32 [72, 16, 2048], P(None, 'lat', 'lon'), may hold values from -7 to 6
- sound_coef: float32 [72], replicated, may hold values from 0.5 to 2
- inverse: float32 [144, 144], replicated
Outputs:
- updated: bfloat16 [6, 72, 512, 2048], P(None, None, 'lat', 'lon')
All inputs are finite; a program needn't handle non-finite values.
Results may differ from a plain program's by a relative error of at most 0.0065.
Values may be sent and summed in bfloat16 or wider, within the bound.
A program may use at most 128 MiB of HBM per device.

v0:
```python
import functools

import jax
import jax.numpy as jnp
from jax import lax
from jax.experimental import pallas as pl
from jax.experimental.pallas import tpu as pltpu
from jax.sharding import PartitionSpec as P

MESH = pl.DeviceIdType.MESH
HALO = 8
ROWS = 32
COLS = 128
GROUP = 8
FAR = -100000
OWNER = 1000
PAIRS = ((0, 1), (2, 5), (3, 4))
F32 = jnp.float32
BF16 = jnp.bfloat16


def cubic_weights(fraction):
    return (
        -fraction * (fraction - 1.0) * (fraction - 2.0) / 6.0,
        (fraction + 1.0) * (fraction - 1.0) * (fraction - 2.0) / 2.0,
        -(fraction + 1.0) * fraction * (fraction - 2.0) / 2.0,
        (fraction + 1.0) * fraction * (fraction - 1.0) / 6.0,
    )


def chunks_of(pair, groups):
    cuts, first = [], 0
    while first < groups:
        size = min(3, groups - first)
        if pair == len(PAIRS) - 1 and groups - first <= 3:
            size = 1
        cuts.append((first, size))
        first += size
    return cuts


def iota(shape, dim):
    return lax.broadcasted_iota(jnp.int32, shape, dim)


def taps(distance, weights):
    out = jnp.where(distance == 3, weights[3], 0.0)
    for node in (2, 1, 0):
        out = jnp.where(distance == node, weights[node], out)
    return out


def kernel(
    levels, bands, sectors,
    fields, frac_lat, off_lat, frac_lon, off_lon, sound, inverse, out,
    x, send_up, send_down, low, high, packed, send_right, send_left, from_left, from_right,
    send_corner, corner, merged, lat_w, lat_anchor, lat_matrix, lon_w, lon_anchor, lon_matrix,
    result, u, v, v_low, v_high, edge_right, edge_left, u_west, u_east, rhs, solved, acoustic,
    in_sem, out_sem, send_sem, recv_sem,
):
    groups = levels // GROUP
    doubles = (groups + 1) // 2
    a = lax.axis_index("lat")
    s = lax.axis_index("lon")
    up, down = lax.rem(a + 1, bands), lax.rem(a + bands - 1, bands)
    right, left = lax.rem(s + 1, sectors), lax.rem(s + sectors - 1, sectors)

    loads = [
        pltpu.make_async_copy(fields.at[f], x.at[f], in_sem.at[f]) for f in range(6)
    ]
    for pair in PAIRS:
        for f in pair:
            loads[f].start()

    barrier = pltpu.get_barrier_semaphore()
    for there in (
        (down, s), (up, s), (a, left), (a, right),
        (down, left), (down, right), (up, left), (up, right),
    ):
        pl.semaphore_signal(barrier, inc=1, device_id=there, device_id_type=MESH)

    sent = []

    def send(src, dst, there):
        k = len(sent)
        copy = pltpu.make_async_remote_copy(
            src_ref=src, dst_ref=dst, send_sem=send_sem.at[k], recv_sem=recv_sem.at[k],
            device_id=there, device_id_type=MESH,
        )
        copy.start()
        sent.append(copy)
        return copy

    def pack_rows(p):
        fa, fb = PAIRS[p]

        def body(g, carry):
            for q in range(GROUP):
                l = g * GROUP + q
                xa, xb = x[fa, l].astype(F32), x[fb, l].astype(F32)
                send_up[p, l] = jnp.concatenate([xa[24:32], xb[24:32]], 0).astype(BF16)
                send_down[p, l] = jnp.concatenate([xa[0:8], xb[0:8]], 0).astype(BF16)
            return carry

        lax.fori_loop(0, groups, body, 0)

    lane64 = iota((2 * ROWS, COLS), 1)
    even64 = (lane64 & 8) == 0

    def pack_columns(p):
        fa, fb = PAIRS[p]

        def body(g, carry):
            acc = jnp.zeros((2 * ROWS, COLS), F32)
            for q in range(GROUP):
                l = g * GROUP + q
                both = jnp.concatenate([x[fa, l], x[fb, l]], 0).astype(F32)
                turned = pltpu.roll(both, (8 + 16 * q) % COLS, 1)
                acc = jnp.where((lane64 >= 16 * q) & (lane64 < 16 * q + 16), turned, acc)
            packed[g] = acc
            return carry

        lax.fori_loop(0, groups, body, 0)
        if groups % 2:
            packed[groups] = jnp.zeros((2 * ROWS, COLS), F32)

        def merge(d, carry):
            first, second = packed[2 * d], packed[2 * d + 1]
            to_right = jnp.where(even64, first, pltpu.roll(second, 8, 1))
            to_left = jnp.where(even64, pltpu.roll(second, COLS - 8, 1), first)
            send_right[p, d] = to_right.astype(BF16)
            send_left[p, d] = to_left.astype(BF16)
            for c, (block, row) in enumerate(
                ((to_left, 0), (to_right, 0), (to_left, 24), (to_right, 24))
            ):
                send_corner[c, p, d] = jnp.concatenate(
                    [block[row : row + 8], block[row + 32 : row + 40]], 0
                ).astype(BF16)
            return carry

        lax.fori_loop(0, doubles, merge, 0)

    lat_copies, lon_copies = {}, {}
    for p, (fa, fb) in enumerate(PAIRS):
        loads[fa].wait()
        loads[fb].wait()
        pack_rows(p)
        if p == 0:
            pl.semaphore_wait(barrier, 8)
        for k, (first, size) in enumerate(chunks_of(p, groups)):
            span = pl.ds(first * GROUP, size * GROUP)
            lat_copies[p, k] = (
                send(send_up.at[p, span], low.at[p, span], (up, s)),
                send(send_down.at[p, span], high.at[p, span], (down, s)),
            )
            if k == 0:
                pack_columns(p)
                lon_copies[p] = [
                    send(send_right.at[p], from_left.at[p], (a, right)),
                    send(send_left.at[p], from_right.at[p], (a, left)),
                ]
                for c, there in enumerate(
                    ((down, left), (down, right), (up, left), (up, right))
                ):
                    lon_copies[p].append(send(send_corner.at[c, p], corner.at[c, p], there))

    lane_row = iota(lat_anchor.shape, 1)
    rounded = [w.astype(BF16).astype(F32) for w in cubic_weights(frac_lat[...])]
    for node in range(4):
        lat_w[node] = rounded[node]
    lat_anchor[...] = off_lat[...] + (lane_row & 31) + (HALO - 1) + ((lane_row & 32) >> 5) * OWNER
    rounded = [w.astype(BF16).astype(F32) for w in cubic_weights(frac_lon[...])]
    for node in range(4):
        lon_w[node] = rounded[node]
    lon_anchor[...] = off_lon[...] + iota(lon_anchor.shape, 1) + (HALO - 1)

    r = iota((96, COLS), 0)
    own = jnp.where(r < 32, r + HALO, r - 32 + HALO + OWNER)
    below = jnp.where(r < 72, r - 64, r - 72 + OWNER)
    above = jnp.where(r < 88, r - 80 + HALO + ROWS, r - 88 + HALO + ROWS + OWNER)
    below = jnp.where(a == 0, FAR, below)
    above = jnp.where(a == bands - 1, FAR, above)
    row_place = jnp.where(r < 64, own, jnp.where(r < 80, below, above))

    def build_lat(j, carry):
        distance = row_place - lat_anchor[pl.ds(j, 1), :]
        turned = taps(distance, [lat_w[node, pl.ds(j, 1), :] for node in range(4)]).T.astype(BF16)
        lat_matrix[2 * j] = turned[0:64]
        lat_matrix[2 * j + 1] = turned[64:128]
        return carry

    lax.fori_loop(0, levels // 2, build_lat, 0)

    place = iota((COLS, COLS), 0) + HALO
    r16 = iota((16, COLS), 0)
    left_first = jnp.where(r16 < 8, r16, r16 - 8 + HALO + COLS)
    right_first = jnp.where(r16 < 8, r16 + HALO + COLS, r16 - 8)

    def build_lon(g, carry):
        edge_place = jnp.where((g & 1) == 0, left_first, right_first)
        for q in range(GROUP):
            l = g * GROUP + q
            anchor = lon_anchor[pl.ds(l, 1), :]
            weights = [lon_w[node, pl.ds(l, 1), :] for node in range(4)]
            lon_matrix[l, 0:COLS] = taps(place - anchor, weights).astype(BF16)
            lon_matrix[l, COLS:] = jnp.zeros((COLS, COLS), BF16)
            lon_matrix[l, COLS + 16 * q : COLS + 16 * q + 16] = taps(
                edge_place - anchor, weights
            ).astype(BF16)
        return carry

    lax.fori_loop(0, groups, build_lon, 0)

    inv = inverse[...]
    acoustic[...] = jnp.concatenate([inv, -(inv[:, levels:] * sound[...])], 1).astype(BF16)

    even16 = (iota((16, COLS), 1) & 8) == 0

    def merge_halo(p):
        def body(d, carry):
            l_in, r_in = from_left[p, d].astype(F32), from_right[p, d].astype(F32)
            merged[p, 2 * d, 0:64] = jnp.where(even64, l_in, r_in).astype(BF16)
            merged[p, 2 * d + 1, 0:64] = jnp.where(even64, r_in, l_in).astype(BF16)
            for n, (cl, cr) in enumerate(((3, 2), (1, 0))):
                l_in, r_in = corner[cl, p, d].astype(F32), corner[cr, p, d].astype(F32)
                row = 64 + 16 * n
                merged[p, 2 * d, row : row + 16] = jnp.where(even16, l_in, r_in).astype(BF16)
                merged[p, 2 * d + 1, row : row + 16] = jnp.where(even16, r_in, l_in).astype(BF16)
            return carry

        lax.fori_loop(0, doubles, body, 0)

    writes = []

    def write(f, first, size):
        k = len(writes)
        span = pl.ds(first * GROUP, size * GROUP)
        copy = pltpu.make_async_copy(result.at[f, span], out.at[f, span], out_sem.at[k])
        copy.start()
        writes.append(copy)

    def interpolate(p):
        fa, fb = PAIRS[p]
        for k, (first, size) in enumerate(chunks_of(p, groups)):
            for copy in lat_copies[p, k]:
                copy.wait_recv()
            if k == 0:
                for copy in lon_copies[p]:
                    copy.wait_recv()
                merge_halo(p)

            def body(g, carry):
                halo = merged[p, g]
                for q in range(GROUP):
                    l = g * GROUP + q
                    main = jnp.concatenate([x[fa, l], x[fb, l], low[p, l], high[p, l]], 0)
                    y = jnp.dot(
                        lat_matrix[l], jnp.concatenate([main, halo], 1), preferred_element_type=F32
                    ).astype(BF16)
                    z = jnp.dot(y, lon_matrix[l], preferred_element_type=F32).astype(BF16)
                    if p != 1:
                        result[fa, l] = z[0:ROWS]
                        result[fb, l] = z[ROWS:]
                    if p < 2:
                        wide = z.astype(F32)
                        for i in range(0, ROWS, 8):
                            one, two = wide[i : i + 8], wide[ROWS + i : ROWS + i + 8]
                            if p == 0:
                                u[pl.ds(i * levels + l, 8, stride=levels), :] = one
                                v[pl.ds(i * levels + l, 8, stride=levels), :] = two
                            else:
                                at = i * 3 * levels + l
                                rhs[pl.ds(at, 8, stride=3 * levels), :] = one
                                rhs[pl.ds(at + levels, 8, stride=3 * levels), :] = two
                return carry

            lax.fori_loop(first, first + size, body, 0)
            if p != 1:
                write(fa, first, size)
                write(fb, first, size)

    lane = iota((levels, COLS), 1)
    interpolate(0)

    def pack_edges(i, carry):
        block = u[pl.ds(pl.multiple_of(i * levels, 8), levels), :]
        to_right, to_left = carry
        here = lane == i
        return (
            jnp.where(here, pltpu.roll(block, i + 1, 1), to_right),
            jnp.where(here, pltpu.roll(block, i, 1), to_left),
        )

    nothing = jnp.zeros((levels, COLS), F32)
    to_right, to_left = lax.fori_loop(0, ROWS, pack_edges, (nothing, nothing))
    edge_right[...] = to_right
    edge_left[...] = to_left
    edges = [
        send(edge_right, u_west, (a, right)),
        send(edge_left, u_east, (a, left)),
        send(v.at[pl.ds((ROWS - 1) * levels, levels)], v_low, (up, s)),
        send(v.at[pl.ds(0, levels)], v_high, (down, s)),
    ]

    interpolate(1)
    for copy in edges:
        copy.wait_recv()

    v_low[...] = jnp.where(a == 0, 0.0, v_low[...])
    v_high[...] = jnp.where(a == bands - 1, 0.0, v_high[...])

    def diverge(i, south, north):
        block = u[pl.ds(pl.multiple_of(i * levels, 8), levels), :]
        back = lax.rem(COLS - i, COLS)
        west = jnp.where(lane == 0, pltpu.roll(u_west[...], back, 1), pltpu.roll(block, 1, 1))
        east = jnp.where(
            lane == COLS - 1,
            pltpu.roll(u_east[...], COLS - 1 - i, 1),
            pltpu.roll(block, COLS - 1, 1),
        )
        at = pl.multiple_of(i * 3 * levels + 2 * levels, 8)
        rhs[pl.ds(at, levels), :] = 0.5 * (east - west) + 0.5 * (north - south)

    def v_row(i):
        return v[pl.ds(pl.multiple_of(i * levels, 8), levels), :]

    diverge(0, v_low[...], v_row(1))

    def inner(i, carry):
        diverge(i, v_row(i - 1), v_row(i + 1))
        return carry

    lax.fori_loop(1, ROWS - 1, inner, 0)
    diverge(ROWS - 1, v_row(ROWS - 2), v_high[...])

    def solve(h, carry):
        at = pl.multiple_of(2 * h * 3 * levels, 8)
        both = jnp.concatenate(
            [rhs[pl.ds(at, 3 * levels), :], rhs[pl.ds(at + 3 * levels, 3 * levels), :]], 1
        ).astype(BF16)
        answer = jnp.dot(acoustic[...], both, preferred_element_type=F32)
        for c in range(0, 2 * levels, 8):
            solved[pl.ds(c * ROWS + 2 * h, 8, stride=ROWS), :] = answer[c : c + 8, :COLS]
            solved[pl.ds(c * ROWS + 2 * h + 1, 8, stride=ROWS), :] = answer[c : c + 8, COLS:]
        return carry

    lax.fori_loop(0, ROWS // 2, solve, 0)

    def round_off(g, carry):
        for q in range(GROUP):
            l = g * GROUP + q
            result[2, l] = solved[pl.ds(pl.multiple_of(l * ROWS, ROWS), ROWS), :].astype(BF16)
            result[5, l] = solved[
                pl.ds(pl.multiple_of((l + levels) * ROWS, ROWS), ROWS), :
            ].astype(BF16)
        return carry

    lax.fori_loop(0, groups, round_off, 0)
    write(2, 0, groups)
    write(5, 0, groups)

    interpolate(2)
    for copy in sent:
        copy.wait_send()
    for copy in writes:
        copy.wait()


def local(bands, sectors, fields, frac_lat, off_lat, frac_lon, off_lon, sound_coef, inverse):
    levels = fields.shape[1]
    groups = levels // GROUP
    doubles = (groups + 1) // 2

    def twice(block):
        block = block[:, 0, :]
        return jnp.concatenate([block, block], 1).reshape(levels // 2, COLS)

    vmem = pl.BlockSpec(memory_space=pltpu.VMEM)
    anywhere = pl.BlockSpec(memory_space=pl.ANY)
    halo_rows = pltpu.VMEM((3, levels, 16, COLS), BF16)
    halo_columns = pltpu.VMEM((3, doubles, 2 * ROWS, COLS), BF16)
    corners = pltpu.VMEM((4, 3, doubles, 16, COLS), BF16)
    level_rows = pltpu.VMEM((levels, COLS), F32)
    whole = pltpu.VMEM((ROWS * levels, COLS), F32)
    messages = 2 * sum(len(chunks_of(p, groups)) for p in range(3)) + 18 + 4
    outgoing = 2 * len(chunks_of(0, groups)) + 2 * len(chunks_of(2, groups)) + 2
    return pl.pallas_call(
        functools.partial(kernel, levels, bands, sectors),
        out_shape=jax.ShapeDtypeStruct(fields.shape, BF16),
        in_specs=[anywhere] + [vmem] * 6,
        out_specs=anywhere,
        scratch_shapes=[
            pltpu.VMEM(fields.shape, BF16),
            halo_rows, halo_rows, halo_rows, halo_rows,
            pltpu.VMEM((2 * doubles, 2 * ROWS, COLS), F32),
            halo_columns, halo_columns, halo_columns, halo_columns,
            corners, corners,
            pltpu.VMEM((3, 2 * doubles, 96, COLS), BF16),
            pltpu.VMEM((4, levels // 2, COLS), F32),
            pltpu.VMEM((levels // 2, COLS), jnp.int32),
            pltpu.VMEM((levels, 64, 96), BF16),
            pltpu.VMEM((4, levels, COLS), F32),
            pltpu.VMEM((levels, COLS), jnp.int32),
            pltpu.VMEM((levels, 2 * COLS, COLS), BF16),
            pltpu.VMEM(fields.shape, BF16),
            whole, whole,
            level_rows, level_rows, level_rows, level_rows, level_rows, level_rows,
            pltpu.VMEM((3 * ROWS * levels, COLS), F32),
            pltpu.VMEM((2 * ROWS * levels, COLS), F32),
            pltpu.VMEM((2 * levels, 3 * levels), BF16),
            pltpu.SemaphoreType.DMA((6,)),
            pltpu.SemaphoreType.DMA((outgoing,)),
            pltpu.SemaphoreType.DMA((messages,)),
            pltpu.SemaphoreType.DMA((messages,)),
        ],
        compiler_params=pltpu.CompilerParams(
            collective_id=0, has_side_effects=True, vmem_limit_bytes=48 * 2**20
        ),
        cost_estimate=pl.CostEstimate(
            flops=10**9, bytes_accessed=2 * 2 * fields.size, transcendentals=0
        ),
    )(
        fields, twice(frac_lat), twice(off_lat), frac_lon[:, 0, :], off_lon[:, 0, :],
        sound_coef[None, :], inverse,
    )


def solution(mesh):
    placed = (
        P(None, None, "lat", "lon"),
        P(None, "lon", "lat"),
        P(None, "lon", "lat"),
        P(None, "lat", "lon"),
        P(None, "lat", "lon"),
        P(),
        P(),
    )
    return jax.shard_map(
        functools.partial(local, mesh.shape["lat"], mesh.shape["lon"]),
        mesh=mesh, in_specs=placed, out_specs=P(None, None, "lat", "lon"), check_vma=False,
    )
```

profile of v0, /device:TPU:8, one launch (start us, length us, event | category | flops | bytes accessed | tf_op | source)
XLA Modules:
  0.0 52.5 jit_solution(1251816570605327557)
XLA Ops:
  0.0 0.8 %pad_maximum_fusion = f32[72,64]{0,1:T(8,128)S(1)} fusion(f32[72,32]{0,1:T(8,128)} %bitcast.8), kind=kLoop, calls=%fused_computation | loop fusion | flops 4608 | bytes 27648 | tf_op jit(solution)/shard_map/concatenate | solution.py:376
  0.8 0.1 copy.10
  0.9 0.1 reshape.6.frac_lat
  1.0 0.8 %pad_add_fusion = s32[72,64]{0,1:T(8,128)S(1)} fusion(s32[72,32]{0,1:T(8,128)} %bitcast.9), kind=kLoop, calls=%fused_computation.1 | loop fusion | flops 4608 | bytes 27648 | tf_op jit(solution)/shard_map/concatenate | solution.py:376
  1.8 0.1 copy.11
  1.8 0.1 reshape.7.off_lat
  1.9 0.0 copy-start
  1.9 0.9 %copy-done = f32[144,144]{1,0:T(8,128)S(1)} copy-done((f32[144,144]{1,0:T(8,128)S(1)}, f32[144,144]{1,0:T(8,128)}, u32[]{:S(2)}) %copy-start) | copy-done | bytes 82968
  2.8 0.0 copy-start.1
  2.8 0.8 %copy-done.1 = f32[72,1,128]{2,1,0:T(1,128)S(1)} copy-done((f32[72,1,128]{2,1,0:T(1,128)S(1)}, f32[72,1,128]{2,1,0:T(1,128)}, u32[]{:S(2)}) %copy-start.1) | copy-done | bytes 36888
  3.6 0.0 copy-start.2
  3.6 0.8 %copy-done.2 = s32[72,1,128]{2,1,0:T(1,128)S(1)} copy-done((s32[72,1,128]{2,1,0:T(1,128)S(1)}, s32[72,1,128]{2,1,0:T(1,128)}, u32[]{:S(2)}) %copy-start.2) | copy-done | bytes 36888
  4.4 0.0 copy-start.3
  4.4 0.7 %copy-done.3 = f32[72]{0:T(128)S(1)} copy-done((f32[72]{0:T(128)S(1)}, f32[72]{0:T(128)}, u32[]{:S(2)}) %copy-start.3) | copy-done | bytes 312
  5.0 45.7 %shard_map.73 = bf16[6,72,32,128]{3,2,1,0:T(8,128)(2,1)S(1)} custom-call(bf16[6,72,32,128]{3,2,1,0:T(8,128)(2,1)} %fields.1, f32[36,128]{1,0:T(8,128)S(1)} %reshape.6.frac_lat, s32[36,128]{1,0:T(8,128)S(1)} %reshape.7.off_lat, f32[72,128]{1,0:T(8,128)S(1)} %bitcast.5, s32[72,128]{1,0:T(8,128)S(1)} %bitcast.6, f32[1,72]{1,0:T(1,128)S(1)} %bitcast.7, ...), custom_call_target="tpu_custom_call" | custom-call | flops 1000000000 | bytes 7077888 | tf_op jit(solution)/shard_map/pallas_call | solution.py:387
  50.7 1.8 %copy.13 = bf16[6,72,32,128]{3,2,1,0:T(8,128)(2,1)} copy(bf16[6,72,32,128]{3,2,1,0:T(8,128)(2,1)S(1)} %shard_map.73) | data formatting | bytes 7077888
Async XLA Ops:
  1.9 0.9 %copy-start = (f32[144,144]{1,0:T(8,128)S(1)}, f32[144,144]{1,0:T(8,128)}, u32[]{:S(2)}) copy-start(f32[144,144]{1,0:T(8,128)} %inverse.1) | copy-start | bytes 248836
  2.8 0.8 %copy-start.1 = (f32[72,1,128]{2,1,0:T(1,128)S(1)}, f32[72,1,128]{2,1,0:T(1,128)}, u32[]{:S(2)}) copy-start(f32[72,1,128]{2,1,0:T(1,128)} %param.10) | copy-start | bytes 110596
  3.6 0.8 %copy-start.2 = (s32[72,1,128]{2,1,0:T(1,128)S(1)}, s32[72,1,128]{2,1,0:T(1,128)}, u32[]{:S(2)}) copy-start(s32[72,1,128]{2,1,0:T(1,128)} %param.11) | copy-start | bytes 110596
  4.4 0.7 %copy-start.3 = (f32[72]{0:T(128)S(1)}, f32[72]{0:T(128)}, u32[]{:S(2)}) copy-start(f32[72]{0:T(128)} %param.12) | copy-start | bytes 868
where the time goes:
time: 53 us; the launch traced here: 52.5 us
  Pallas kernels  45.7 us (86%)
  local copies, waits for them, and re-layouts  5.21 us (10%)
  other arithmetic  1.61 us (3%)
    pallas_call x1, Pallas kernels, local(): pl.pallas_call(functools.partial(kernel, levels, bands, sectors), out_sha...  45.7 us
    unnamed x9, local copies, waits for them, and re-layouts  4.91 us
    concatenate x2, other arithmetic, twice(): return jnp.concatenate([block, block], 1).reshape(levels // 2, COLS)  1.61 us

commit v1 on v0

v1 whole, which is shorter than its diff:
```python
import functools

import jax
import jax.numpy as jnp
from jax import lax
from jax.experimental import pallas as pl
from jax.experimental.pallas import tpu as pltpu
from jax.sharding import PartitionSpec as P

MESH = pl.DeviceIdType.MESH
HALO = 8
ROWS = 32
COLS = 128
GROUP = 8
FAR = -100000
PAIRS = ((0, 1), (2, 5), (3, 4))
F32 = jnp.float32
BF16 = jnp.bfloat16
LON = BF16
PIECES = 2


def cubic_weights(fraction):
    return (
        -fraction * (fraction - 1.0) * (fraction - 2.0) / 6.0,
        (fraction + 1.0) * (fraction - 1.0) * (fraction - 2.0) / 2.0,
        -(fraction + 1.0) * fraction * (fraction - 2.0) / 2.0,
        (fraction + 1.0) * fraction * (fraction - 1.0) / 6.0,
    )


def chunks_of(pair, groups):
    cuts, first = [], 0
    while first < groups:
        size = min(3, groups - first)
        if pair == len(PAIRS) - 1 and groups - first <= 3:
            size = 1
        cuts.append((first, size))
        first += size
    return cuts


def iota(shape, dim):
    return lax.broadcasted_iota(jnp.int32, shape, dim)


def taps(distance, weights):
    out = jnp.where(distance == 3, weights[3], jnp.zeros((), weights[3].dtype))
    for node in (2, 1, 0):
        out = jnp.where(distance == node, weights[node], out)
    return out


def kernel(
    levels, bands, sectors,
    fields, frac_lat, off_lat, frac_lon, off_lon, sound, inverse, final,
    out, x, frac_lat_in, off_lat_in, frac_lon_in, off_lon_in, sound_in, inverse_in,
    frac_lat_t, off_lat_t,
    send_up, send_down, low, high, picker, packed, send_right, send_left, from_left, from_right,
    send_corner, corner, merged, lat_w, lat_anchor, lat_matrix, lon_w, lon_anchor, lon_matrix,
    interim, u, v, v_first, v_last, v_low, v_high, edge_right, edge_left, u_west, u_east, u_edges,
    rhs, solved, acoustic, slope,
    in_sem, out_sem, send_sem, recv_sem,
):
    groups = levels // GROUP
    doubles = (groups + 1) // 2
    u_step, rhs_step, solved_step = levels + 1, 3 * levels + 1, ROWS + 1
    a = lax.axis_index("lat")
    s = lax.axis_index("lon")
    up, down = lax.rem(a + 1, bands), lax.rem(a + bands - 1, bands)
    right, left = lax.rem(s + 1, sectors), lax.rem(s + sectors - 1, sectors)

    started = []

    def load(src, dst):
        copy = pltpu.make_async_copy(src, dst, in_sem.at[len(started)])
        copy.start()
        started.append(copy)
        return copy

    loads = {}
    for p, pair in enumerate(PAIRS):
        for k, (first, size) in enumerate(chunks_of(p, groups) if p == 0 else [(0, groups)]):
            span = pl.ds(first * GROUP, size * GROUP)
            loads[p, k] = [load(fields.at[f, span], x.at[f, span]) for f in pair]
    small = [
        load(src, dst)
        for src, dst in (
            (frac_lon.at[:, 0, :], frac_lon_in), (off_lon.at[:, 0, :], off_lon_in),
            (frac_lat, frac_lat_in), (off_lat, off_lat_in),
            (sound, sound_in), (inverse, inverse_in),
        )
    ]

    barrier = pltpu.get_barrier_semaphore()
    for there in (
        (down, s), (up, s), (a, left), (a, right),
        (down, left), (down, right), (up, left), (up, right),
    ):
        pl.semaphore_signal(barrier, inc=1, device_id=there, device_id_type=MESH)

    sent = []

    def send(src, dst, there):
        k = len(sent)
        copy = pltpu.make_async_remote_copy(
            src_ref=src, dst_ref=dst, send_sem=send_sem.at[k], recv_sem=recv_sem.at[k],
            device_id=there, device_id_type=MESH,
        )
        copy.start()
        sent.append(copy)
        return copy

    def pack_rows(p, first, size):
        fa, fb = PAIRS[p]

        def rows_body(g, carry):
            for q in range(GROUP):
                l = g * GROUP + q
                xa, xb = x[fa, l].astype(F32), x[fb, l].astype(F32)
                send_up[p, l] = jnp.concatenate([xa[24:32], xb[24:32]], 0).astype(BF16)
                send_down[p, l] = jnp.concatenate([xa[0:8], xb[0:8]], 0).astype(BF16)
            return carry

        lax.fori_loop(first, first + size, rows_body, 0)

    def build_picker(t, carry):
        k = iota((2 * COLS, COLS), 0)
        column = k & (COLS - 1)
        q = 2 * t + jnp.where(k >= COLS, 1, 0)
        slot = 16 * (q & 7)
        second = q & 8
        target = jnp.where(
            column >= COLS - HALO,
            slot + second + column - (COLS - HALO),
            jnp.where(column < HALO, COLS + slot + (8 - second) + column, -1),
        )
        lane = iota((2 * COLS, COLS), 1)
        picker[t, :, 0:COLS] = jnp.where(target == lane, 1.0, 0.0).astype(BF16)
        picker[t, :, COLS:] = jnp.where(target == lane + COLS, 1.0, 0.0).astype(BF16)
        return carry

    lax.fori_loop(0, 8, build_picker, 0)

    def pack_columns(pairs):
        for t in range(8):
            rows = []
            for p in pairs:
                for d in range(doubles):
                    l = 16 * d + 2 * t
                    if l < levels:
                        for f in PAIRS[p]:
                            rows.append(jnp.concatenate([x[f, l], x[f, l + 1]], 1))
            part = jnp.dot(jnp.concatenate(rows, 0), picker[t], preferred_element_type=F32)
            at = 0
            for p in pairs:
                for d in range(doubles):
                    if 16 * d + 2 * t < levels:
                        block = part[at : at + 2 * ROWS]
                        at += 2 * ROWS
                        packed[p, d] = block if t == 0 else packed[p, d] + block
        for p in pairs:

            def merge(d, carry):
                block = packed[p, d]
                to_right, to_left = block[:, :COLS], block[:, COLS:]
                send_right[p, d] = to_right.astype(BF16)
                send_left[p, d] = to_left.astype(BF16)
                for c, (side, row) in enumerate(
                    ((to_left, 0), (to_right, 0), (to_left, 24), (to_right, 24))
                ):
                    send_corner[c, p, d] = jnp.concatenate(
                        [side[row : row + 8], side[row + 32 : row + 40]], 0
                    ).astype(BF16)
                return carry

            lax.fori_loop(0, doubles, merge, 0)

    lat_copies, lon_copies = {}, {}

    def send_rows(p, k, first, size):
        span = pl.ds(first * GROUP, size * GROUP)
        lat_copies[p, k] = (
            send(send_up.at[p, span], low.at[p, span], (up, s)),
            send(send_down.at[p, span], high.at[p, span], (down, s)),
        )

    def send_columns(p):
        lon_copies[p] = [
            send(send_corner.at[c, p], corner.at[c, p], there)
            for c, there in enumerate(((down, left), (down, right), (up, left), (up, right)))
        ]
        lon_copies[p].append(send(send_right.at[p], from_left.at[p], (a, right)))
        lon_copies[p].append(send(send_left.at[p], from_right.at[p], (a, left)))

    for k, (first, size) in enumerate(chunks_of(0, groups)):
        for copy in loads[0, k]:
            copy.wait()
        pack_rows(0, first, size)
        if k == 0:
            pl.semaphore_wait(barrier, 8)
        send_rows(0, k, first, size)
    pack_columns([0])
    send_columns(0)
    for p in (1, 2):
        for copy in loads[p, 0]:
            copy.wait()
        pack_rows(p, 0, groups)
    pack_columns([1, 2])
    for k, (first, size) in enumerate(chunks_of(1, groups)):
        send_rows(1, k, first, size)
    send_columns(1)
    send_columns(2)
    for copy in small:
        copy.wait()

    rounded = [w.astype(BF16).astype(F32) for w in cubic_weights(frac_lon_in[...])]
    for node in range(4):
        lon_w[node] = rounded[node]
    lon_anchor[...] = (off_lon_in[...] + iota(lon_anchor.shape, 1) + (HALO - 1)).astype(F32)

    place = (iota((COLS, COLS), 0) + HALO).astype(F32).astype(LON)
    r16 = iota((16, COLS), 0)
    left_first = jnp.where(r16 < 8, r16, r16 - 8 + HALO + COLS).astype(F32)
    right_first = jnp.where(r16 < 8, r16 + HALO + COLS, r16 - 8).astype(F32)

    def build_lon(g, carry):
        edge_place = jnp.where((g & 1) == 0, left_first, right_first).astype(LON)
        for q in range(GROUP):
            l = g * GROUP + q
            anchor = jnp.broadcast_to(lon_anchor[pl.ds(l, 1), :], (16, COLS)).astype(LON)
            weights = [
                jnp.broadcast_to(lon_w[node, pl.ds(l, 1), :], (16, COLS)).astype(LON)
                for node in range(4)
            ]
            for t in range(0, COLS, 16):
                lon_matrix[l, t : t + 16] = taps(place[t : t + 16] - anchor, weights).astype(BF16)
            lon_matrix[l, COLS:] = jnp.zeros((COLS, COLS), BF16)
            lon_matrix[l, COLS + 16 * q : COLS + 16 * q + 16] = taps(
                edge_place - anchor, weights
            ).astype(BF16)
        return carry

    lax.fori_loop(0, groups, build_lon, 0)

    frac_lat_t[...] = frac_lat_in[...].T
    off_lat_t[...] = off_lat_in[...].T
    quarter = levels // 4
    lane_row = iota((quarter, COLS), 1)

    def side_by_side(ref):
        total = None
        for q in range(4):
            part = ref[pl.ds(q, quarter, stride=4), :]
            part = jnp.concatenate([part] * 4, 1)
            total = part if total is None else jnp.where(lane_row >= ROWS * q, part, total)
        return total

    rounded = [w.astype(BF16).astype(F32) for w in cubic_weights(side_by_side(frac_lat_t))]
    for node in range(4):
        lat_w[node] = rounded[node]
    lat_anchor[...] = side_by_side(off_lat_t) + (lane_row & (ROWS - 1)) + (HALO - 1)

    r = iota((ROWS + 2 * HALO, COLS), 0)
    below = jnp.where(a == 0, FAR, r - ROWS)
    above = jnp.where(a == bands - 1, FAR, r)
    row_place = jnp.where(r < ROWS, r + HALO, jnp.where(r < ROWS + HALO, below, above))

    def build_lat(h, carry):
        turned = []
        for n in range(3):
            j = 3 * h + n
            distance = row_place - lat_anchor[pl.ds(j, 1), :]
            weights = [lat_w[node, pl.ds(j, 1), :] for node in range(4)]
            turned.append(taps(distance, weights).astype(BF16).T)
        for n in range(3):
            for q in range(4):
                lat_matrix[4 * (3 * h + n) + q] = turned[n][ROWS * q : ROWS * q + ROWS]
        return carry

    lax.fori_loop(0, quarter // 3, build_lat, 0)

    inv = inverse_in[...]
    acoustic[...] = jnp.concatenate([inv, -(inv[:, levels:] * sound_in[...])], 1).astype(BF16)
    k, j = iota(slope.shape, 0), iota(slope.shape, 1)
    minus = ((k < COLS) & (k == j - 1)) | ((k >= COLS) & (k < COLS + ROWS) & (j == 0))
    plus = ((k < COLS) & (k == j + 1)) | (
        (k >= COLS + ROWS) & (k < COLS + 2 * ROWS) & (j == COLS - 1)
    )
    slope[...] = jnp.where(plus, 0.5, jnp.where(minus, -0.5, 0.0)).astype(BF16)

    even64 = (iota((2 * ROWS, COLS), 1) & 8) == 0
    even16 = (iota((16, COLS), 1) & 8) == 0

    def merge_halo(p):
        def halo_body(d, carry):
            l_in, r_in = from_left[p, d].astype(F32), from_right[p, d].astype(F32)
            mine = jnp.where(even64, l_in, r_in), jnp.where(even64, r_in, l_in)
            low_l, low_r = corner[3, p, d].astype(F32), corner[2, p, d].astype(F32)
            high_l, high_r = corner[1, p, d].astype(F32), corner[0, p, d].astype(F32)
            lows = jnp.where(even16, low_l, low_r), jnp.where(even16, low_r, low_l)
            highs = jnp.where(even16, high_l, high_r), jnp.where(even16, high_r, high_l)
            for n in range(2):
                for f in range(2):
                    merged[p, 2 * d + n, f] = jnp.concatenate(
                        [
                            mine[n][ROWS * f : ROWS * f + ROWS],
                            lows[n][8 * f : 8 * f + 8],
                            highs[n][8 * f : 8 * f + 8],
                        ],
                        0,
                    ).astype(BF16)
            return carry

        lax.fori_loop(0, doubles, halo_body, 0)

    def along_lat(p, g):
        fa, fb = PAIRS[p]
        for q in range(GROUP):
            l = g * GROUP + q
            below, above = low[p, l].astype(F32), high[p, l].astype(F32)
            around = [
                jnp.concatenate([below[n : n + 8], above[n : n + 8]], 0).astype(BF16)
                for n in (0, 8)
            ]
            block = jnp.concatenate(
                [
                    jnp.concatenate([x[fa, l], around[0]], 0),
                    merged[p, g, 0],
                    jnp.concatenate([x[fb, l], around[1]], 0),
                    merged[p, g, 1],
                ],
                1,
            )
            y = jnp.dot(lat_matrix[l], block, preferred_element_type=F32).astype(BF16)
            interim[q] = jnp.concatenate([y[:, : 2 * COLS], y[:, 2 * COLS :]], 0)

    def along_lon(p, g):
        fa, fb = PAIRS[p]
        for q in range(GROUP):
            l = g * GROUP + q
            z = jnp.dot(interim[q], lon_matrix[l], preferred_element_type=F32).astype(BF16)
            one, two = z[:ROWS], z[ROWS:]
            if p != 1:
                out[fa, l] = one
                out[fb, l] = two
            if p < 2:
                one, two = one.astype(F32), two.astype(F32)
                for i in range(0, ROWS, 8):
                    if p == 0:
                        u[pl.ds(i * u_step + l, 8, stride=u_step), :] = one[i : i + 8]
                        v[pl.ds((i + 1) * u_step + l, 8, stride=u_step), :] = two[i : i + 8]
                    else:
                        at = i * rhs_step + l
                        rhs[pl.ds(at, 8, stride=rhs_step), :] = one[i : i + 8]
                        rhs[pl.ds(at + levels, 8, stride=rhs_step), :] = two[i : i + 8]

    writes = []

    def write(f, first, size):
        span = pl.ds(first * GROUP, size * GROUP)
        copy = pltpu.make_async_copy(out.at[f, span], final.at[f, span], out_sem.at[len(writes)])
        copy.start()
        writes.append(copy)

    def interpolate(p, chunks):
        for k in chunks:
            first, size = chunks_of(p, groups)[k]
            if k == 0:
                for copy in lon_copies[p]:
                    copy.wait_recv()
                merge_halo(p)
            for copy in lat_copies[p, k]:
                copy.wait_recv()
            if k == 0:
                along_lat(p, 0)

            def cells_body(g, carry):
                along_lon(p, g - 1)
                along_lat(p, g)
                return carry

            lax.fori_loop(max(first, 1), first + size, cells_body, 0)
            done = first + size
            if done == groups:
                along_lon(p, groups - 1)
            else:
                done = done - 1
            if p == 2:
                for f in PAIRS[p]:
                    write(f, max(first - 1, 0), done - max(first - 1, 0))

    lane = iota((levels, COLS), 1)
    interpolate(0, range(len(chunks_of(0, groups))))
    write(0, 0, groups)
    write(1, 0, groups)

    def pack_edges(h, carry):
        to_right, to_left = carry
        for n in range(4):
            i = 4 * h + n
            turned = pltpu.roll(u[pl.ds(i * u_step, levels), :], i + 1, 1)
            to_right = jnp.where(lane == i, turned, to_right)
            to_left = jnp.where(lane == i + 1, turned, to_left)
        return to_right, to_left

    nothing = jnp.zeros((levels, COLS), F32)
    to_right, to_left = lax.fori_loop(0, ROWS // 4, pack_edges, (nothing, nothing))
    edge_right[...] = to_right
    edge_left[...] = pltpu.roll(to_left, ROWS - 1, 1)
    v_first[...] = v[u_step : u_step + levels]
    v_last[...] = v[ROWS * u_step : ROWS * u_step + levels]
    edges = [
        send(edge_right, u_west, (a, right)),
        send(edge_left, u_east, (a, left)),
        send(v_last, v_low, (up, s)),
        send(v_first, v_high, (down, s)),
    ]
    count = len(chunks_of(1, groups))
    interpolate(1, range(1))
    for k, (first, size) in enumerate(chunks_of(2, groups)):
        send_rows(2, k, first, size)
    interpolate(1, range(1, count - 1))
    for copy in edges:
        copy.wait_recv()

    v[0:levels] = jnp.where(a == 0, 0.0, v_low[...])
    v[(ROWS + 1) * u_step : (ROWS + 1) * u_step + levels] = jnp.where(
        a == bands - 1, 0.0, v_high[...]
    )
    u_edges[...] = jnp.where(lane < ROWS, u_west[...], u_east[...])

    def diverge(h, carry):
        changes = []
        for m in range(2):
            blocks = []
            for n in range(4):
                i = 8 * h + 4 * m + n
                mine = (lane == i) | (lane == i + ROWS)
                blocks.append(
                    jnp.concatenate(
                        [u[pl.ds(i * u_step, levels), :], jnp.where(mine, u_edges[...], 0.0)], 1
                    )
                )
            changes.append(
                jnp.dot(
                    jnp.concatenate(blocks, 0).astype(BF16), slope[...], preferred_element_type=F32
                )
            )
        for m in range(2):
            for n in range(4):
                i = 8 * h + 4 * m + n
                south = v[pl.ds(i * u_step, levels), :]
                north = v[pl.ds((i + 2) * u_step, levels), :]
                rhs[pl.ds(i * rhs_step + 2 * levels, levels), :] = (
                    changes[m][n * levels : (n + 1) * levels] + 0.5 * (north - south)
                )
        return carry

    lax.fori_loop(0, ROWS // 8, diverge, 0)
    interpolate(1, range(count - 1, count))

    def solve(h, carry):
        for m in range(4):
            i = 8 * h + 2 * m
            both = jnp.concatenate(
                [
                    rhs[pl.ds(i * rhs_step, 3 * levels), :],
                    rhs[pl.ds((i + 1) * rhs_step, 3 * levels), :],
                ],
                1,
            ).astype(BF16)
            answer = jnp.dot(acoustic[...], both, preferred_element_type=F32)
            for c in range(0, 2 * levels, 8):
                at = c * solved_step + i
                solved[pl.ds(at, 8, stride=solved_step), :] = answer[c : c + 8, :COLS]
                solved[pl.ds(at + 1, 8, stride=solved_step), :] = answer[c : c + 8, COLS:]
        return carry

    lax.fori_loop(0, ROWS // 8, solve, 0)

    def round_off(g, carry):
        for q in range(GROUP):
            l = g * GROUP + q
            out[2, l] = solved[pl.ds(l * solved_step, ROWS), :].astype(BF16)
            out[5, l] = solved[pl.ds((l + levels) * solved_step, ROWS), :].astype(BF16)
        return carry

    lax.fori_loop(0, groups, round_off, 0)
    write(2, 0, groups)
    write(5, 0, groups)

    interpolate(2, range(len(chunks_of(2, groups))))
    for copy in sent:
        copy.wait_send()
    for copy in writes:
        copy.wait()


def hand_over(src, dst, held, in_sem, out_sem):
    size = src.shape[1] // PIECES
    pieces = [(f, pl.ds(n * size, size)) for f in range(6) for n in range(PIECES)]
    reads = [
        pltpu.make_async_copy(src.at[f, span], held.at[f, span], in_sem.at[k])
        for k, (f, span) in enumerate(pieces)
    ]
    writes = [
        pltpu.make_async_copy(held.at[f, span], dst.at[f, span], out_sem.at[k])
        for k, (f, span) in enumerate(pieces)
    ]
    for copy in reads:
        copy.start()
    for read, copy in zip(reads, writes):
        read.wait()
        copy.start()
    for copy in writes:
        copy.wait()


def local(bands, sectors, fields, frac_lat, off_lat, frac_lon, off_lon, sound_coef, inverse):
    levels = fields.shape[1]
    groups = levels // GROUP
    doubles = (groups + 1) // 2
    outside = pl.BlockSpec(memory_space=pltpu.HBM)
    halo_rows = pltpu.VMEM((3, levels, 16, COLS), BF16)
    halo_columns = pltpu.VMEM((3, doubles, 2 * ROWS, COLS), BF16)
    corners = pltpu.VMEM((4, 3, doubles, 16, COLS), BF16)
    level_rows = pltpu.VMEM((levels, COLS), F32)
    messages = 2 * sum(len(chunks_of(p, groups)) for p in range(3)) + 18 + 4
    outgoing = 4 + 2 * len(chunks_of(2, groups))
    stepped = pl.pallas_call(
        functools.partial(kernel, levels, bands, sectors),
        out_shape=jax.ShapeDtypeStruct(fields.shape, BF16),
        in_specs=[outside] * 7,
        out_specs=outside,
        scratch_shapes=[
            pltpu.VMEM(fields.shape, BF16),
            pltpu.VMEM(fields.shape, BF16),
            pltpu.VMEM((ROWS, levels), F32),
            pltpu.VMEM((ROWS, levels), jnp.int32),
            pltpu.VMEM((levels, COLS), F32),
            pltpu.VMEM((levels, COLS), jnp.int32),
            pltpu.VMEM((1, levels), F32),
            pltpu.VMEM((2 * levels, 2 * levels), F32),
            pltpu.VMEM((levels, ROWS), F32),
            pltpu.VMEM((levels, ROWS), jnp.int32),
            halo_rows, halo_rows, halo_rows, halo_rows,
            pltpu.VMEM((8, 2 * COLS, 2 * COLS), BF16),
            pltpu.VMEM((3, doubles, 2 * ROWS, 2 * COLS), F32),
            halo_columns, halo_columns, halo_columns, halo_columns,
            corners, corners,
            pltpu.VMEM((3, 2 * doubles, 2, ROWS + 2 * HALO, COLS), BF16),
            pltpu.VMEM((4, levels // 4, COLS), F32),
            pltpu.VMEM((levels // 4, COLS), jnp.int32),
            pltpu.VMEM((levels, ROWS, ROWS + 2 * HALO), BF16),
            pltpu.VMEM((4, levels, COLS), F32),
            level_rows,
            pltpu.VMEM((levels, 2 * COLS, COLS), BF16),
            pltpu.VMEM((GROUP, 2 * ROWS, 2 * COLS), BF16),
            pltpu.VMEM((ROWS * (levels + 1), COLS), F32),
            pltpu.VMEM(((ROWS + 2) * (levels + 1), COLS), F32),
        ]
        + [level_rows] * 9
        + [
            pltpu.VMEM((ROWS * (3 * levels + 1), COLS), F32),
            pltpu.VMEM((2 * levels * (ROWS + 1), COLS), F32),
            pltpu.VMEM((2 * levels, 3 * levels), BF16),
            pltpu.VMEM((2 * COLS, COLS), BF16),
            pltpu.SemaphoreType.DMA((4 + 2 * len(chunks_of(0, groups)) + 6,)),
            pltpu.SemaphoreType.DMA((outgoing,)),
            pltpu.SemaphoreType.DMA((messages,)),
            pltpu.SemaphoreType.DMA((messages,)),
        ],
        compiler_params=pltpu.CompilerParams(
            collective_id=0, has_side_effects=True, vmem_limit_bytes=60 * 2**20
        ),
        cost_estimate=pl.CostEstimate(
            flops=10**9, bytes_accessed=2 * 2 * fields.size, transcendentals=0
        ),
    )(
        fields, frac_lat[:, 0, :].T, off_lat[:, 0, :].T, frac_lon, off_lon,
        sound_coef[None, :], inverse,
    )
    return pl.pallas_call(
        hand_over,
        out_shape=jax.ShapeDtypeStruct(fields.shape, BF16),
        in_specs=[outside],
        out_specs=outside,
        scratch_shapes=[
            pltpu.VMEM(fields.shape, BF16),
            pltpu.SemaphoreType.DMA((6 * PIECES,)),
            pltpu.SemaphoreType.DMA((6 * PIECES,)),
        ],
        compiler_params=pltpu.CompilerParams(vmem_limit_bytes=60 * 2**20),
    )(stepped)


def solution(mesh):
    placed = (
        P(None, None, "lat", "lon"),
        P(None, "lon", "lat"),
        P(None, "lon", "lat"),
        P(None, "lat", "lon"),
        P(None, "lat", "lon"),
        P(),
        P(),
    )
    return jax.shard_map(
        functools.partial(local, mesh.shape["lat"], mesh.shape["lon"]),
        mesh=mesh, in_specs=placed, out_specs=P(None, None, "lat", "lon"), check_vma=False,
    )
```

time: 53 us -> 35.3 us (0.67)
  the two profiles are of different devices: /device:TPU:8 before, /device:TPU:0 now
where the time goes in v1:
time: 35.3 us; the launch traced here: 35.2 us
  Pallas kernels  35.2 us (100%)
    pallas_call x1, Pallas kernels, local(): pl.pallas_call(functools.partial(kernel, levels, bands, sectors), out_sha...  32.1 us
    pallas_call x1, Pallas kernels, local(): pl.pallas_call(hand_over, out_shape=jax.ShapeDtypeStruct(fields.shape, BF...  3.08 us

profile of v1, /device:TPU:0, one launch (start us, length us, event | category | flops | bytes accessed | tf_op | source)
XLA Modules:
  0.0 35.2 jit_solution(12948395961830856724)
XLA Ops:
  0.0 32.1 %shard_map.73.src = bf16[6,72,32,128]{3,2,1,0:T(8,128)(2,1)} custom-call(bf16[6,72,32,128]{3,2,1,0:T(8,128)(2,1)} %fields.1, f32[32,72]{1,0:T(8,128)} %bitcast.7, s32[32,72]{1,0:T(8,128)} %bitcast.8, f32[72,1,128]{2,1,0:T(1,128)} %frac_lon.1, s32[72,1,128]{2,1,0:T(1,128)} %off_lon.1, f32[1,72]{1,0:T(1,128)} %bitcast.9, f32[144,144]{1,0:T(8,128)} %inverse.1), custom_call_target="tpu_custom_call" | custom-call | flops 1000000000 | bytes 7077888 | tf_op jit(solution)/shard_map/pallas_call | solution.py:531
  32.1 3.1 %shard_map.74 = bf16[6,72,32,128]{3,2,1,0:T(8,128)(2,1)} custom-call(bf16[6,72,32,128]{3,2,1,0:T(8,128)(2,1)} %shard_map.73.src), custom_call_target="tpu_custom_call" | custom-call | tf_op jit(solution)/shard_map/pallas_call | solution.py:584

commit v2 on v1

--- a/solution.py
+++ b/solution.py
@@ -17,7 +17,7 @@
 F32 = jnp.float32
 BF16 = jnp.bfloat16
 LON = BF16
-PIECES = 2
+PIECES = 1
 
 
 def cubic_weights(fraction):
@@ -199,14 +199,16 @@
         pack_rows(0, first, size)
         if k == 0:
             pl.semaphore_wait(barrier, 8)
-        send_rows(0, k, first, size)
+            send_rows(0, k, first, size)
     pack_columns([0])
     send_columns(0)
+    send_rows(0, 1, *chunks_of(0, groups)[1])
     for p in (1, 2):
         for copy in loads[p, 0]:
             copy.wait()
         pack_rows(p, 0, groups)
     pack_columns([1, 2])
+    send_rows(0, 2, *chunks_of(0, groups)[2])
     for k, (first, size) in enumerate(chunks_of(1, groups)):
         send_rows(1, k, first, size)
     send_columns(1)
@@ -391,21 +393,23 @@
                     write(f, max(first - 1, 0), done - max(first - 1, 0))
 
     lane = iota((levels, COLS), 1)
+    for k, (first, size) in enumerate(chunks_of(2, groups)):
+        send_rows(2, k, first, size)
     interpolate(0, range(len(chunks_of(0, groups))))
     write(0, 0, groups)
     write(1, 0, groups)
 
     def pack_edges(h, carry):
         to_right, to_left = carry
-        for n in range(4):
-            i = 4 * h + n
+        for n in range(8):
+            i = 8 * h + n
             turned = pltpu.roll(u[pl.ds(i * u_step, levels), :], i + 1, 1)
             to_right = jnp.where(lane == i, turned, to_right)
             to_left = jnp.where(lane == i + 1, turned, to_left)
         return to_right, to_left
 
     nothing = jnp.zeros((levels, COLS), F32)
-    to_right, to_left = lax.fori_loop(0, ROWS // 4, pack_edges, (nothing, nothing))
+    to_right, to_left = lax.fori_loop(0, ROWS // 8, pack_edges, (nothing, nothing))
     edge_right[...] = to_right
     edge_left[...] = pltpu.roll(to_left, ROWS - 1, 1)
     v_first[...] = v[u_step : u_step + levels]
@@ -417,10 +421,9 @@
         send(v_first, v_high, (down, s)),
     ]
     count = len(chunks_of(1, groups))
-    interpolate(1, range(1))
-    for k, (first, size) in enumerate(chunks_of(2, groups)):
-        send_rows(2, k, first, size)
-    interpolate(1, range(1, count - 1))
+    interpolate(1, range(count - 1))
+    interpolate(1, range(count - 1, count))
+    interpolate(2, range(4))
     for copy in edges:
         copy.wait_recv()
 
@@ -458,7 +461,6 @@
         return carry
 
     lax.fori_loop(0, ROWS // 8, diverge, 0)
-    interpolate(1, range(count - 1, count))
 
     def solve(h, carry):
         for m in range(4):
@@ -490,7 +492,7 @@
     write(2, 0, groups)
     write(5, 0, groups)
 
-    interpolate(2, range(len(chunks_of(2, groups))))
+    interpolate(2, range(4, len(chunks_of(2, groups))))
     for copy in sent:
         copy.wait_send()
     for copy in writes:

time: 35.3 us -> 31.7 us (0.90)
  the two profiles are of different devices: /device:TPU:0 before, /device:TPU:8 now
where the time goes in v2:
time: 31.7 us; the launch traced here: 31.6 us
  Pallas kernels  31.6 us (100%)
    pallas_call x1, Pallas kernels, local(): pl.pallas_call(functools.partial(kernel, levels, bands, sectors), out_sha...  28.6 us
    pallas_call x1, Pallas kernels, local(): pl.pallas_call(hand_over, out_shape=jax.ShapeDtypeStruct(fields.shape, BF...  2.95 us

profile of v2, /device:TPU:8, one launch (start us, length us, event | category | flops | bytes accessed | tf_op | source)
XLA Modules:
  0.0 31.6 jit_solution(682335276442469373)
XLA Ops:
  0.0 28.6 %shard_map.73.src = bf16[6,72,32,128]{3,2,1,0:T(8,128)(2,1)} custom-call(bf16[6,72,32,128]{3,2,1,0:T(8,128)(2,1)} %fields.1, f32[32,72]{1,0:T(8,128)} %bitcast.7, s32[32,72]{1,0:T(8,128)} %bitcast.8, f32[72,1,128]{2,1,0:T(1,128)} %frac_lon.1, s32[72,1,128]{2,1,0:T(1,128)} %off_lon.1, f32[1,72]{1,0:T(1,128)} %bitcast.9, f32[144,144]{1,0:T(8,128)} %inverse.1), custom_call_target="tpu_custom_call" | custom-call | flops 1000000000 | bytes 7077888 | tf_op jit(solution)/shard_map/pallas_call | solution.py:533
  28.7 3.0 %shard_map.74 = bf16[6,72,32,128]{3,2,1,0:T(8,128)(2,1)} custom-call(bf16[6,72,32,128]{3,2,1,0:T(8,128)(2,1)} %shard_map.73.src), custom_call_target="tpu_custom_call" | custom-call | tf_op jit(solution)/shard_map/pallas_call | solution.py:586

commit v3 on v2

--- a/solution.py
+++ b/solution.py
@@ -435,10 +435,10 @@
 
     def diverge(h, carry):
         changes = []
-        for m in range(2):
+        for m in range(4):
             blocks = []
             for n in range(4):
-                i = 8 * h + 4 * m + n
+                i = 16 * h + 4 * m + n
                 mine = (lane == i) | (lane == i + ROWS)
                 blocks.append(
                     jnp.concatenate(
@@ -450,9 +450,9 @@
                     jnp.concatenate(blocks, 0).astype(BF16), slope[...], preferred_element_type=F32
                 )
             )
-        for m in range(2):
+        for m in range(4):
             for n in range(4):
-                i = 8 * h + 4 * m + n
+                i = 16 * h + 4 * m + n
                 south = v[pl.ds(i * u_step, levels), :]
                 north = v[pl.ds((i + 2) * u_step, levels), :]
                 rhs[pl.ds(i * rhs_step + 2 * levels, levels), :] = (
@@ -460,11 +460,11 @@
                 )
         return carry
 
-    lax.fori_loop(0, ROWS // 8, diverge, 0)
+    lax.fori_loop(0, ROWS // 16, diverge, 0)
 
     def solve(h, carry):
-        for m in range(4):
-            i = 8 * h + 2 * m
+        for m in range(8):
+            i = 16 * h + 2 * m
             both = jnp.concatenate(
                 [
                     rhs[pl.ds(i * rhs_step, 3 * levels), :],
@@ -479,7 +479,7 @@
                 solved[pl.ds(at + 1, 8, stride=solved_step), :] = answer[c : c + 8, COLS:]
         return carry
 
-    lax.fori_loop(0, ROWS // 8, solve, 0)
+    lax.fori_loop(0, ROWS // 16, solve, 0)
 
     def round_off(g, carry):
         for q in range(GROUP):

time: 31.7 us -> 31 us (0.978)
  Pallas kernels: 31.6 us -> 30.9 us
    pallas_call x1, Pallas kernels: 28.6 us -> 28 us  [local(): pl.pallas_call(functools.partial(kernel, levels, bands, sectors), out_sha...]
where the time goes in v3:
time: 31 us; the launch traced here: 30.9 us
  Pallas kernels  30.9 us (100%)
    pallas_call x1, Pallas kernels, local(): pl.pallas_call(functools.partial(kernel, levels, bands, sectors), out_sha...  28 us
    pallas_call x1, Pallas kernels, local(): pl.pallas_call(hand_over, out_shape=jax.ShapeDtypeStruct(fields.shape, BF...  2.95 us

profile of v3, /device:TPU:8, one launch (start us, length us, event | category | flops | bytes accessed | tf_op | source)
XLA Modules:
  0.0 30.9 jit_solution(931604360017357092)
XLA Ops:
  0.0 28.0 %shard_map.73.src = bf16[6,72,32,128]{3,2,1,0:T(8,128)(2,1)} custom-call(bf16[6,72,32,128]{3,2,1,0:T(8,128)(2,1)} %fields.1, f32[32,72]{1,0:T(8,128)} %bitcast.7, s32[32,72]{1,0:T(8,128)} %bitcast.8, f32[72,1,128]{2,1,0:T(1,128)} %frac_lon.1, s32[72,1,128]{2,1,0:T(1,128)} %off_lon.1, f32[1,72]{1,0:T(1,128)} %bitcast.9, f32[144,144]{1,0:T(8,128)} %inverse.1), custom_call_target="tpu_custom_call" | custom-call | flops 1000000000 | bytes 7077888 | tf_op jit(solution)/shard_map/pallas_call | solution.py:533
  28.0 3.0 %shard_map.74 = bf16[6,72,32,128]{3,2,1,0:T(8,128)(2,1)} custom-call(bf16[6,72,32,128]{3,2,1,0:T(8,128)(2,1)} %shard_map.73.src), custom_call_target="tpu_custom_call" | custom-call | tf_op jit(solution)/shard_map/pallas_call | solution.py:586
